TPU v7x, 32 devices: a whole 2x2x4 slice. The times are simulated.
32 devices in a mesh: dp: 4 (over y, core), section: 2 (over x), tensor: 4 (over z).
Axes of the slice: x: 2, y: 2, z: 4, core: 2. Of those that a mesh axis runs over, the one named last changes fastest.
Arguments:
- saved_input: bfloat16 [2, 2, 512, 8192], P('section', None, ('dp', 'tensor')), may hold values from -6 to 6
- kv_grad: bfloat16 [2, 2, 512, 2048], P('section', None, 'dp', 'tensor'), may hold values from -1.5 to 1.5
- kv_weight: bfloat16 [2, 8192, 2048], P('section', 'dp', 'tensor'), may hold values from -0.0625 to 0.0625
- norm_gain: bfloat16 [2, 8192], P('section'), may hold values from 0.5 to 1.5
- top_grad: bfloat16 [2, 512, 8192], P(None, ('dp', 'tensor')), may hold values from -1.5 to 1.5
- noise_salt: int32 [1], replicated, may hold values from 0 to 1073741823
- step_counter: int32 [1], replicated, may hold values from 0 to 999999
Outputs:
- input_grads: bfloat16 [2, 2, 512, 8192], P('section', None, ('dp', 'tensor'))
- weight_grads: float32 [2, 8192, 2048], P('section', 'dp', 'tensor')
All inputs are finite; a program needn't handle non-finite values.
Results may differ from a plain program's by a relative error of at most 0.012.
Values may be sent and summed in bfloat16 or wider, within the bound.
A program may use at most 128 MiB of HBM per device.

v0:
```python
import jax
import jax.numpy as jnp
from jax import lax
from jax.sharding import PartitionSpec as P


def entering(shard, axis, join, neutral):
    count = lax.axis_size(axis)
    place = lax.axis_index(axis)
    ahead = count - 1 - place
    gathered = lax.all_gather(shard.astype(jnp.bfloat16), axis)
    state = jnp.zeros_like(shard) + jnp.asarray(neutral, shard.dtype)

    def one(lap, state):
        source = count - 1 - lap
        return join(state, lax.dynamic_index_in_dim(gathered, source, 0, False).astype(shard.dtype))

    return lax.fori_loop(0, ahead, one, state)


def mix_bits(salt, counter, layer, group, index):
    h = (
        index * jnp.int32(-1640531535)
        + salt * jnp.int32(374761393)
        + counter * jnp.int32(668265263)
    )
    h = h + layer * jnp.int32(-1028477379) + group * jnp.int32(1274126177)
    h = h ^ lax.shift_right_logical(h, jnp.int32(16))
    h = h * jnp.int32(2146121005)
    h = h ^ lax.shift_right_logical(h, jnp.int32(15))
    h = h * jnp.int32(-2073254261)
    h = h ^ lax.shift_right_logical(h, jnp.int32(16))
    return lax.shift_right_logical(h, jnp.int32(8)).astype(jnp.float32) * (1.0 / 16777216.0)


def dither(term, salt, counter, layer, group, index):
    noise = mix_bits(salt, counter, layer, group, index)
    moved = term * (1.0 + (noise - 0.5) * 0.5)
    return lax.optimization_barrier(moved.astype(jnp.bfloat16)).astype(jnp.float32)


def add_pair(earlier, later):
    return earlier + later


def shards(saved_input, kv_grad, kv_weight, norm_gain, top_grad, noise_salt, step_counter):
    salt = noise_salt[0]
    counter = step_counter[0]
    layer = lax.axis_index("section")
    group_p = lax.axis_index("dp")
    cotan = kv_grad[0]
    weight = kv_weight[0]
    width_t = weight.shape[1]
    total_cols = width_t * lax.axis_size("tensor")
    col_start = lax.axis_index("tensor") * jnp.int32(width_t)
    input_float = saved_input[0].astype(jnp.float32)
    inverse_scale = lax.rsqrt(jnp.mean(input_float * input_float, axis=-1, keepdims=True) + 1e-05)
    centered_input = input_float * inverse_scale
    gain_float = norm_gain[0].astype(jnp.float32)
    normed_values = (centered_input * gain_float).astype(jnp.bfloat16)
    normed_all = lax.all_gather(normed_values, "tensor", axis=1, tiled=True)
    partial_grad = jnp.einsum(
        "mtk,dk->mtd",
        cotan,
        lax.all_gather(weight, "dp", axis=0, tiled=True),
        preferred_element_type=jnp.float32,
    )
    normed_grad = lax.psum_scatter(
        partial_grad.astype(jnp.bfloat16), "tensor", scatter_dimension=1, tiled=True
    ).astype(jnp.float32)
    hidden_gradient = normed_grad * gain_float
    branch_path = inverse_scale * (
        hidden_gradient
        - centered_input * jnp.mean(hidden_gradient * centered_input, axis=-1, keepdims=True)
    )
    later = entering(branch_path, "section", add_pair, jnp.zeros_like(branch_path))
    grad_in = (top_grad.astype(jnp.float32) + branch_path + later).astype(jnp.bfloat16)
    term = jnp.einsum("mtd,mtk->dk", normed_all, cotan, preferred_element_type=jnp.float32)
    row_ids = jnp.arange(weight.shape[0] * lax.axis_size("dp"), dtype=jnp.int32)
    index = (
        row_ids[:, None] * jnp.int32(total_cols)
        + col_start
        + jnp.arange(width_t, dtype=jnp.int32)[None, :]
    )
    wsum = lax.psum_scatter(
        dither(term, salt, counter, layer, group_p, index).astype(jnp.bfloat16),
        "dp",
        scatter_dimension=0,
        tiled=True,
    ).astype(jnp.float32)
    return (grad_in[None], wsum[None])


def solution(mesh):
    placed = (
        P("section", None, ("dp", "tensor"), None),
        P("section", None, "dp", "tensor"),
        P("section", "dp", "tensor"),
        P("section", None),
        P(None, ("dp", "tensor"), None),
        P(),
        P(),
    )
    return jax.shard_map(
        shards,
        mesh=mesh,
        in_specs=placed,
        out_specs=(P("section", None, ("dp", "tensor"), None), P("section", "dp", "tensor")),
        check_vma=False,
    )
```

profile of v0, /device:TPU:0, one launch (start us, length us, event | category | flops | bytes accessed | tf_op | source)
XLA Modules:
  0.0 358.5 jit_solution(3302901762300414112)
XLA Ops:
  7.2 0.0 all-gather.8.cloned.1.call-start
  7.2 0.7 all-gather.8.cloned.1.call-update
  7.9 0.0 reduce-scatter.3.cloned.1.call-start
  8.0 62.6 %all-gather.8.cloned.1.call-done = bf16[1,8192,512]{2,1,0:T(8,128)(2,1)} async-done(((bf16[1,2048,512]{2,1,0:T(8,128)(2,1)}), bf16[1,8192,512]{2,1,0:T(8,128)(2,1)}) %all-gather.8.cloned.1.call-update) | async-done | bytes 8388624 | tf_op jit(solution)/shard_map/all_gather | solution.py:65
  70.6 7.8 %convolution_convert_fusion = bf16[2,128,8192]{2,1,0:T(8,128)(2,1)} fusion(bf16[1,8192,512]{2,1,0:T(8,128)(2,1)} %all-gather.8.cloned.1.call-done, bf16[1,2,128,512]{3,2,1,0:T(8,128)(2,1)S(1)} %copy-done), kind=kOutput, calls=%fused_computation.14 | convolution fusion | flops 2149580800 | bytes 12845056 | tf_op jit(solution)/shard_map/mtk,dk->mtd/dot_general | solution.py:62
  78.4 0.0 reduce-scatter.3.cloned.1.call-update
  78.4 0.0 all-gather.6.cloned.1.call-start
  78.4 0.7 copy-done.3
  79.2 0.4 copy-done.1
  79.6 0.3 fusion.18
  79.9 75.4 %reduce-scatter.3.cloned.1.call-done = bf16[2,32,8192]{2,1,0:T(8,128)(2,1)} async-done(((bf16[2,128,8192]{2,1,0:T(8,128)(2,1)}), bf16[2,32,8192]{2,1,0:T(8,128)(2,1)}) %reduce-scatter.3.cloned.1.call-update) | async-done | bytes 1048592 | tf_op jit(solution)/shard_map/reduce_scatter | solution.py:68
  155.3 2.9 fusion.17
  158.3 0.0 all-gather.10.cloned.1.call-start
  159.7 1.5 fusion.19
  161.2 0.0 reduce-scatter.5.cloned.1.call-start
  161.3 78.4 %all-gather.6.cloned.1.call-done = bf16[2,128,8192]{2,1,0:T(8,128)(2,1)} async-done(((bf16[2,32,8192]{2,1,0:T(8,128)(2,1)}), bf16[2,128,8192]{2,1,0:T(8,128)(2,1)}) %all-gather.6.cloned.1.call-update) | async-done | bytes 4194320 | tf_op jit(solution)/shard_map/all_gather | solution.py:61
  239.7 16.4 %fusion.9 = bf16[8192,512]{1,0:T(8,128)(2,1)} fusion(bf16[2,128,8192]{2,1,0:T(8,128)(2,1)} %all-gather.6.cloned.1.call-done, s32[]{:T(128)S(6)} %mul.124, s32[]{:T(128)S(6)} %mul.123, s32[]{:T(128)} %bitcast.11, s32[]{:T(128)} %bitcast.10, s32[8192]{0:T(1024)S(1)} %multiply_add_fusion, bf16[1,2,128,512]{3,2,1,0:T(8,128)(2,1)S(1)} %copy-done), kind=kOutput, calls=%fused_computation.13 | convolution fusion | flops 2239758336 | bytes 12877840 | tf_op jit(solution)/shard_map/mtd,mtk->dk/dot_general | solution.py:78
  256.1 17.3 %all-gather.10.cloned.1.call-done = bf16[4,32,8192]{2,1,0:T(8,128)(2,1)} async-done(((bf16[2,32,8192]{2,1,0:T(8,128)(2,1)}), bf16[4,32,8192]{2,1,0:T(8,128)(2,1)}) %all-gather.10.cloned.1.call-update) | async-done | bytes 2097168 | tf_op jit(solution)/shard_map/all_gather | solution.py:11
  273.4 0.1 broadcast_in_dim.18
  273.6 1.7 while.12
  273.6 1.7 convert_add_fusion.2
  275.3 3.3 fusion.20
  278.5 69.2 %reduce-scatter.5.cloned.1.call-done = bf16[2048,512]{1,0:T(8,128)(2,1)} async-done(((bf16[8192,512]{1,0:T(8,128)(2,1)}), bf16[2048,512]{1,0:T(8,128)(2,1)}) %reduce-scatter.5.cloned.1.call-update) | async-done | bytes 2097168 | tf_op jit(solution)/shard_map/reduce_scatter | solution.py:85
  347.8 4.2 %bitcast_convert_fusion = f32[1,2048,512]{2,1,0:T(8,128)} fusion(bf16[2048,512]{1,0:T(8,128)(2,1)} %reduce-scatter.5.cloned.1.call-done), kind=kLoop, calls=%fused_computation.26 | loop fusion | flops 1048576 | bytes 6291456 | tf_op jit(solution)/shard_map/broadcast_in_dim | solution.py:91
  (13 shorter events, 0.1 us)
Async XLA Ops:
  7.2 63.4 %copy-start = (bf16[1,2,128,512]{3,2,1,0:T(8,128)(2,1)S(1)}, bf16[1,2,128,512]{3,2,1,0:T(8,128)(2,1)}, u32[]{:S(2)}) copy-start(bf16[1,2,128,512]{3,2,1,0:T(8,128)(2,1)} %param.10) | copy-start | bytes 786436
  7.2 63.4 %all-gather.8.cloned.1.call-start = ((), (), s32[]{:S(2)}) async-start(), calls=%async_computation.5 | async-start | bytes 10485760 | tf_op jit(solution)/shard_map/all_gather | solution.py:65
  7.9 147.4 %reduce-scatter.3.cloned.1.call-start = ((), (), s32[]{:S(2)}) async-start(), calls=%async_computation.2 | async-start | bytes 5242880 | tf_op jit(solution)/shard_map/reduce_scatter | solution.py:68
  78.4 0.8 copy-start.3
  78.4 1.2 copy-start.1
  78.4 161.3 %all-gather.6.cloned.1.call-start = ((), (), s32[]{:S(2)}) async-start(), calls=%async_computation.3 | async-start | bytes 5242880 | tf_op jit(solution)/shard_map/all_gather | solution.py:61
  155.3 4.3 %copy-start.2 = (bf16[2,32,8192]{2,1,0:T(8,128)(2,1)S(1)}, bf16[2,32,8192]{2,1,0:T(8,128)(2,1)}, u32[]{:S(2)}) copy-start(bf16[2,32,8192]{2,1,0:T(8,128)(2,1)} %reduce-scatter.3.cloned.1.call-done) | copy-start | bytes 3145732
  158.3 115.1 %all-gather.10.cloned.1.call-start = ((), (), s32[]{:S(2)}) async-start(), calls=%async_computation.6 | async-start | bytes 3145728 | tf_op jit(solution)/shard_map/all_gather | solution.py:11
  161.2 186.6 %reduce-scatter.5.cloned.1.call-start = ((), (), s32[]{:S(2)}) async-start(), calls=%async_computation.4 | async-start | bytes 10485760 | tf_op jit(solution)/shard_map/reduce_scatter | solution.py:85
Sparse Core Ops, SparseCore 0:
  9.6 60.9 all-gather.7
  78.5 76.7 reduce-scatter.2
  158.4 81.2 all-gather.5
  241.7 31.6 all-gather.9
  276.0 71.7 reduce-scatter.4
where the time goes:
time: 359 us
  waiting for transfers between devices  304 us (85%)
  matrix products  24.2 us (7%)
  between operations  15.1 us (4%)
  other arithmetic  14 us (4%)
    all_gather x1, waiting for transfers between devices, shards(): normed_all = lax.all_gather(normed_values, 'tensor', axis=1, tiled=True)  78.4 us
    reduce_scatter x1, waiting for transfers between devices, shards(): lax.psum_scatter(partial_grad.astype(jnp.bfloat16), 'tensor', scatter_dim...  75.4 us
    reduce_scatter x1, waiting for transfers between devices, shards(): lax.psum_scatter(dither(term, salt, counter, layer, group_p, index).astyp...  69.2 us
    all_gather x1, waiting for transfers between devices, shards(): lax.all_gather(weight, 'dp', axis=0, tiled=True)  62.6 us
    all_gather x1, waiting for transfers between devices, entering(): gathered = lax.all_gather(shard.astype(jnp.bfloat16), axis)  17.3 us
    dot_general x1, matrix products, shards(): jnp.einsum('mtd,mtk->dk', normed_all, cotan, preferred_element_type=jnp.f...  16.4 us
    dot_general x1, matrix products, shards(): jnp.einsum('mtk,dk->mtd', cotan, lax.all_gather(weight, 'dp', axis=0, til...  7.77 us
    broadcast_in_dim x2, other arithmetic, shards(): return (grad_in[None], wsum[None])  7.47 us
  transfers between devices with their start and end apart: 5, of which 5 were waited for; matrix products, arithmetic and copies ran while one was open for 7% of the time, Pallas kernels for 0%

commit v1 on v0

--- a/solution.py
+++ b/solution.py
@@ -58,16 +58,22 @@
     centered_input = input_float * inverse_scale
     gain_float = norm_gain[0].astype(jnp.float32)
     normed_values = (centered_input * gain_float).astype(jnp.bfloat16)
-    normed_all = lax.all_gather(normed_values, "tensor", axis=1, tiled=True)
-    partial_grad = jnp.einsum(
-        "mtk,dk->mtd",
-        cotan,
-        lax.all_gather(weight, "dp", axis=0, tiled=True),
-        preferred_element_type=jnp.float32,
+    n_dp = lax.axis_size("dp")
+    n_tensor = lax.axis_size("tensor")
+    micro, tok, feats = normed_values.shape
+    rows = weight.shape[0]
+    cotan_all = lax.all_gather(cotan, "dp", axis=0)
+    parts = jnp.einsum("pmtk,dk->pmtd", cotan_all, weight, preferred_element_type=jnp.float32)
+    mine = lax.psum_scatter(
+        parts.astype(jnp.bfloat16), "tensor", scatter_dimension=2, tiled=True
     )
-    normed_grad = lax.psum_scatter(
-        partial_grad.astype(jnp.bfloat16), "tensor", scatter_dimension=1, tiled=True
-    ).astype(jnp.float32)
+    mine = lax.all_to_all(mine, "dp", split_axis=0, concat_axis=0, tiled=True)
+    normed_grad = (
+        mine.astype(jnp.float32).transpose(1, 2, 0, 3).reshape(micro, tok, feats)
+    )
+    sliced = normed_values.reshape(micro, tok, n_dp, rows).transpose(2, 0, 1, 3)
+    sliced = lax.all_to_all(sliced, "dp", split_axis=0, concat_axis=0, tiled=True)
+    normed_all = lax.all_gather(sliced, "tensor", axis=2, tiled=True)
     hidden_gradient = normed_grad * gain_float
     branch_path = inverse_scale * (
         hidden_gradient
@@ -75,19 +81,18 @@
     )
     later = entering(branch_path, "section", add_pair, jnp.zeros_like(branch_path))
     grad_in = (top_grad.astype(jnp.float32) + branch_path + later).astype(jnp.bfloat16)
-    term = jnp.einsum("mtd,mtk->dk", normed_all, cotan, preferred_element_type=jnp.float32)
-    row_ids = jnp.arange(weight.shape[0] * lax.axis_size("dp"), dtype=jnp.int32)
+    row_ids = group_p * rows + jnp.arange(rows, dtype=jnp.int32)
     index = (
         row_ids[:, None] * jnp.int32(total_cols)
         + col_start
         + jnp.arange(width_t, dtype=jnp.int32)[None, :]
     )
-    wsum = lax.psum_scatter(
-        dither(term, salt, counter, layer, group_p, index).astype(jnp.bfloat16),
-        "dp",
-        scatter_dimension=0,
-        tiled=True,
-    ).astype(jnp.float32)
+    wsum = jnp.zeros((rows, width_t), jnp.float32)
+    for p in range(n_dp):
+        term = jnp.einsum(
+            "mtd,mtk->dk", normed_all[p], cotan_all[p], preferred_element_type=jnp.float32
+        )
+        wsum = wsum + dither(term, salt, counter, layer, jnp.int32(p), index)
     return (grad_in[None], wsum[None])
 
 

time: 359 us -> 286 us (0.80)
  waiting for transfers between devices: 304 us -> 207 us
  local copies, waits for them, and re-layouts: 1.28 us -> 14 us
  starting transfers between devices: 0.2 us -> 8.66 us
  other arithmetic: 14 us -> 19.9 us
    reduce_scatter x2 -> x1, waiting for transfers between devices: 145 us -> 76.9 us  [shards(): lax.psum_scatter(parts.astype(jnp.bfloat16), 'tensor', scatter_dimension=...]
    all_gather x2, waiting for transfers between devices: 141 us -> 94.4 us  [the longest x1 73.3 us: shards(): normed_all = lax.all_gather(sliced, 'tensor', axis=2, tiled=True)]
    all_to_all x0 -> x2, waiting for transfers between devices: none -> 21.1 us  [the longest x1 11.3 us: shards(): mine = lax.all_to_all(mine, 'dp', split_axis=0, concat_axis=0, tiled=True)]
    all_to_all x0 -> x2, starting transfers between devices: none -> 8.5 us  [the longest x1 4.26 us: shards(): lax.all_to_all(sliced, 'dp', split_axis=0, concat_axis=0, tiled=True)]
    reshape x0 -> x2, local copies, waits for them, and re-layouts: none -> 7.04 us  [shards(): mine.astype(jnp.float32).transpose(1, 2, 0, 3).reshape(micro, tok, feats)]
    transpose x0 -> x1, other arithmetic: none -> 4.5 us  [shards(): sliced = normed_values.reshape(micro, tok, n_dp, rows).transpose(2, 0, 1, 3)]
    dot_general x2 -> x5, matrix products: 24.2 us -> 21.2 us  [the longest x4 15.5 us: shards(): jnp.einsum('mtd,mtk->dk', normed_all[p], cotan_all[p], preferred_element_...]
  transfers between devices with their start and end apart: 5 -> 6, of which waited for: 5 -> 6; matrix products, arithmetic and copies ran while one was open for 7% -> 5% of each run, Pallas kernels for 0% -> 0%
where the time goes in v1:
time: 286 us
  waiting for transfers between devices  207 us (72%)
  matrix products  21.2 us (7%)
  other arithmetic  19.9 us (7%)
  between operations  15.2 us (5%)
  local copies, waits for them, and re-layouts  14 us (5%)
  starting transfers between devices  8.66 us (3%)
    reduce_scatter x1, waiting for transfers between devices, shards(): lax.psum_scatter(parts.astype(jnp.bfloat16), 'tensor', scatter_dimension=...  76.9 us
    all_gather x1, waiting for transfers between devices, shards(): normed_all = lax.all_gather(sliced, 'tensor', axis=2, tiled=True)  73.3 us
    all_gather x1, waiting for transfers between devices, shards(): cotan_all = lax.all_gather(cotan, 'dp', axis=0)  21.1 us
    dot_general x4, matrix products, shards(): jnp.einsum('mtd,mtk->dk', normed_all[p], cotan_all[p], preferred_element_...  15.5 us
    all_gather x1, waiting for transfers between devices, entering(): gathered = lax.all_gather(shard.astype(jnp.bfloat16), axis)  14 us
    all_to_all x1, waiting for transfers between devices, shards(): mine = lax.all_to_all(mine, 'dp', split_axis=0, concat_axis=0, tiled=True)  11.3 us
    all_to_all x1, waiting for transfers between devices, shards(): lax.all_to_all(sliced, 'dp', split_axis=0, concat_axis=0, tiled=True)  9.78 us
    broadcast_in_dim x2, other arithmetic, shards(): return (grad_in[None], wsum[None])  7.29 us
  transfers between devices with their start and end apart: 6, of which 6 were waited for; matrix products, arithmetic and copies ran while one was open for 5% of the time, Pallas kernels for 0%

profile of v1, /device:TPU:0, one launch (start us, length us, event | category | flops | bytes accessed | tf_op | source)
XLA Modules:
  0.0 286.0 jit_solution(7158111046641820395)
XLA Ops:
  8.0 21.1 %all-gather.4.cloned.1.call-done = bf16[4,2,128,512]{3,2,1,0:T(8,128)(2,1)} async-done(((bf16[1,2,128,512]{3,2,1,0:T(8,128)(2,1)}), bf16[4,2,128,512]{3,2,1,0:T(8,128)(2,1)}) %all-gather.4.cloned.1.call-update) | async-done | bytes 1048592 | tf_op jit(solution)/shard_map/all_gather | solution.py:65
  29.0 5.6 %convolution_convert_fusion = bf16[4,2,128,2048]{3,2,1,0:T(8,128)(2,1)} fusion(bf16[4,2,128,512]{3,2,1,0:T(8,128)(2,1)} %all-gather.4.cloned.1.call-done, bf16[1,2048,512]{2,1,0:T(8,128)(2,1)S(1)} %copy-done), kind=kOutput, calls=%fused_computation.55 | convolution fusion | flops 2149580800 | bytes 7340032 | tf_op jit(solution)/shard_map/pmtk,dk->pmtd/dot_general | solution.py:66
  34.7 76.9 %reduce-scatter.2.cloned.1.call-done = bf16[4,2,32,2048]{3,2,1,0:T(8,128)(2,1)} async-done(((bf16[4,2,128,2048]{3,2,1,0:T(8,128)(2,1)}), bf16[4,2,32,2048]{3,2,1,0:T(8,128)(2,1)}) %reduce-scatter.2.cloned.1.call-update) | async-done | bytes 1048592 | tf_op jit(solution)/shard_map/reduce_scatter | solution.py:67
  111.6 4.2 %all-to-all-start = ((bf16[4,2,32,2048]{3,2,1,0:T(8,128)(2,1)}), bf16[4,2,32,2048]{3,2,1,0:T(8,128)(2,1)}, u32[]{:S(2)}, u32[]{:S(2)}) async-start(bf16[4,2,32,2048]{3,2,1,0:T(8,128)(2,1)} %reduce-scatter.2.cloned.1.call-done), calls=%async_computation.1 | async-start | bytes 2097152 | tf_op jit(solution)/shard_map/all_to_all | solution.py:70
  115.9 2.7 reshape.72
  119.1 11.3 %all-to-all-done = bf16[4,2,32,2048]{3,2,1,0:T(8,128)(2,1)} async-done(((bf16[4,2,32,2048]{3,2,1,0:T(8,128)(2,1)}), bf16[4,2,32,2048]{3,2,1,0:T(8,128)(2,1)}, u32[]{:S(2)}, u32[]{:S(2)}) %all-to-all-start) | async-done | bytes 1048608 | tf_op jit(solution)/shard_map/all_to_all | solution.py:70
  130.4 2.8 convert_bitcast_fusion
  133.2 2.7 copy.20
  135.9 3.7 %reshape.67 = f32[1,2,32,8192]{3,2,1,0:T(8,128)} reshape(f32[2,32,4,2048]{3,2,1,0:T(4,128)} %copy.20) | data formatting | bytes 4194304 | tf_op jit(solution)/shard_map/reshape | solution.py:72
  139.6 4.5 %fusion.48 = (bf16[4,2,32,2048]{3,2,1,0:T(8,128)(2,1)}, f32[2,32]{1,0:T(2,128)S(1)}) fusion(f32[2,32,4,2048]{3,2,1,0:T(4,128)} %reshape.72, f32[2,32]{1,0:T(2,128)S(1)} %add_rsqrt_fusion, f32[4,2048]{1,0:T(4,128)S(1)} %reshape.71, bf16[4,2,32,2048]{3,2,1,0:T(8,128)(2,1)} %all-to-all-done), kind=kLoop, calls=%fused_computation.72 | loop fusion | flops 3669952 | bytes 4227584 | tf_op jit(solution)/shard_map/transpose | solution.py:74
  144.1 1.5 multiply_convert_fusion.1
  145.6 4.3 %all-to-all-start.1 = ((bf16[4,2,32,2048]{3,2,1,0:T(8,128)(2,1)}), bf16[4,2,32,2048]{3,2,1,0:T(8,128)(2,1)}, u32[]{:S(2)}, u32[]{:S(2)}) async-start(bf16[4,2,32,2048]{3,2,1,0:T(8,128)(2,1)} %get-tuple-element.67), calls=%async_computation.2 | async-start | bytes 2097152 | tf_op jit(solution)/shard_map/all_to_all | solution.py:75
  151.3 3.4 %copy.32 = f32[4,2,4,8,2048]{4,3,0,2,1:T(8,128)} copy(f32[4,2,4,8,2048]{4,3,2,1,0:T(8,128)} %get-tuple-element.69) | data formatting | bytes 4194304 | tf_op jit(solution)/shard_map/reshape | solution.py:72
  154.6 9.8 %all-to-all-done.1 = bf16[4,2,32,2048]{3,2,1,0:T(8,128)(2,1)} async-done(((bf16[4,2,32,2048]{3,2,1,0:T(8,128)(2,1)}), bf16[4,2,32,2048]{3,2,1,0:T(8,128)(2,1)}, u32[]{:S(2)}, u32[]{:S(2)}) %all-to-all-start.1) | async-done | bytes 1048608 | tf_op jit(solution)/shard_map/all_to_all | solution.py:75
  164.4 14.0 %all-gather.6.cloned.1.call-done = bf16[2,2,32,8192]{3,2,1,0:T(8,128)(2,1)} async-done(((bf16[1,2,32,8192]{3,2,1,0:T(8,128)(2,1)}), bf16[2,2,32,8192]{3,2,1,0:T(8,128)(2,1)}) %all-gather.6.cloned.1.call-update) | async-done | bytes 2097168 | tf_op jit(solution)/shard_map/all_gather | solution.py:11
  179.9 3.4 %while.12 = (s32[]{:T(128)}, f32[2,32,8192]{2,1,0:T(8,128)}, s32[]{:T(128)}, bf16[2,2,32,8192]{3,2,1,0:T(8,128)(2,1)}, s32[]{:T(128)}, /*index=5*/s32[]{:T(128)}, s32[]{:T(128)}) while((s32[]{:T(128)}, f32[2,32,8192]{2,1,0:T(8,128)}, s32[]{:T(128)}, bf16[2,2,32,8192]{3,2,1,0:T(8,128)(2,1)}, s32[]{:T(128)}, /*index=5*/s32[]{:T(128)}, ...), condition=%wide.region_4.5_spmd, body=%wide.region_3.4_spmd.sunk | while | flops 1048582 | bytes 5243015 | solution.py:18
  179.9 3.4 %convert_add_fusion.2 = f32[2,32,8192]{2,1,0:T(8,128)} fusion(f32[2,32,8192]{2,1,0:T(8,128)} %get-tuple-element.105, bf16[2,2,32,8192]{3,2,1,0:T(8,128)(2,1)} %get-tuple-element.114, s32[]{:T(128)S(6)} %select_n.8), kind=kLoop, calls=%fused_computation.clone.1 | loop fusion | flops 1048576 | bytes 5242884 | tf_op jit(solution)/shard_map/while/body/add | solution.py:43
  183.3 4.2 %fusion.49 = bf16[1,2,32,8192]{3,2,1,0:T(8,128)(2,1)} fusion(f32[2,32,8192]{2,1,0:T(8,128)} %get-tuple-element.58, bf16[1,2,32,8192]{3,2,1,0:T(8,128)(2,1)S(1)} %copy-done.1, f32[2,32,8192]{2,1,0:T(8,128)} %bitcast.90, bf16[2,32,8192]{2,1,0:T(8,128)(2,1)} %param.13, f32[2,32]{1,0:T(2,128)S(1)} %broadcast_multiply_fusion, f32[8192]{0:T(1024)S(1)} %bitcast.92, ...), kind=kLoop, calls=%fused_computation.73 | loop fusion | flops 5242880 | bytes 7373312 | tf_op jit(solution)/shard_map/broadcast_in_dim | solution.py:96
  187.5 73.3 %all-gather.8.cloned.1.call-done = bf16[4,2,128,2048]{3,2,1,0:T(8,128)(2,1)} async-done(((bf16[4,2,32,2048]{3,2,1,0:T(8,128)(2,1)}), bf16[4,2,128,2048]{3,2,1,0:T(8,128)(2,1)}) %all-gather.8.cloned.1.call-update) | async-done | bytes 4194320 | tf_op jit(solution)/shard_map/all_gather | solution.py:76
  260.8 4.9 %fusion.36 = bf16[2048,512]{1,0:T(8,128)(2,1)S(1)} fusion(s32[]{:T(128)S(6)} %mul.216, s32[]{:T(128)} %bitcast.13, s32[]{:T(128)} %bitcast.12, s32[2048]{0:T(1024)S(1)} %multiply_add_fusion, bf16[4,2,128,2048]{3,2,1,0:T(8,128)(2,1)} %all-gather.8.cloned.1.call-done, bf16[4,2,128,512]{3,2,1,0:T(8,128)(2,1)} %all-gather.4.cloned.1.call-done), kind=kOutput, calls=%fused_computation.51 | convolution fusion | flops 559939584 | bytes 3417092 | tf_op jit(solution)/shard_map/mtd,mtk->dk/dot_general | solution.py:92
  265.7 3.6 %fusion.37 = bf16[2048,512]{1,0:T(8,128)(2,1)S(1)} fusion(s32[]{:T(128)S(6)} %mul.216, s32[]{:T(128)} %bitcast.13, s32[]{:T(128)} %bitcast.12, s32[2048]{0:T(1024)S(1)} %multiply_add_fusion, bf16[4,2,128,2048]{3,2,1,0:T(8,128)(2,1)S(1)} %copy-done.4, bf16[4,2,128,512]{3,2,1,0:T(8,128)(2,1)S(1)} %copy-done.5), kind=kOutput, calls=%fused_computation.52 | convolution fusion | flops 559939584 | bytes 3416076 | tf_op jit(solution)/shard_map/mtd,mtk->dk/dot_general | solution.py:92
  269.3 3.6 %fusion.38 = bf16[2048,512]{1,0:T(8,128)(2,1)S(1)} fusion(s32[]{:T(128)S(6)} %mul.216, s32[]{:T(128)} %bitcast.13, s32[]{:T(128)} %bitcast.12, s32[2048]{0:T(1024)S(1)} %multiply_add_fusion, bf16[4,2,128,2048]{3,2,1,0:T(8,128)(2,1)S(1)} %copy-done.4, bf16[4,2,128,512]{3,2,1,0:T(8,128)(2,1)S(1)} %copy-done.5), kind=kOutput, calls=%fused_computation.53 | convolution fusion | flops 559939584 | bytes 3416076 | tf_op jit(solution)/shard_map/mtd,mtk->dk/dot_general | solution.py:92
  272.9 3.4 %fusion.39 = bf16[2048,512]{1,0:T(8,128)(2,1)S(1)} fusion(s32[]{:T(128)S(6)} %mul.216, s32[]{:T(128)} %bitcast.13, s32[]{:T(128)} %bitcast.12, s32[2048]{0:T(1024)S(1)} %multiply_add_fusion, bf16[4,2,128,2048]{3,2,1,0:T(8,128)(2,1)S(1)} %copy-done.4, bf16[4,2,128,512]{3,2,1,0:T(8,128)(2,1)S(1)} %copy-done.5), kind=kOutput, calls=%fused_computation.54 | convolution fusion | flops 558891008 | bytes 3416076 | tf_op jit(solution)/shard_map/mtd,mtk->dk/dot_general | solution.py:92
  276.4 3.1 %add_bitcast_fusion = f32[1,2048,512]{2,1,0:T(8,128)} fusion(bf16[2048,512]{1,0:T(8,128)(2,1)S(1)} %fusion.36, bf16[2048,512]{1,0:T(8,128)(2,1)S(1)} %fusion.37, bf16[2048,512]{1,0:T(8,128)(2,1)S(1)} %fusion.38, bf16[2048,512]{1,0:T(8,128)(2,1)S(1)} %fusion.39), kind=kLoop, calls=%fused_computation.49 | loop fusion | flops 7340032 | bytes 12582912 | tf_op jit(solution)/shard_map/broadcast_in_dim | solution.py:96
  (28 shorter events, 2.9 us)
Async XLA Ops:
  7.2 21.9 %copy-start = (bf16[1,2048,512]{2,1,0:T(8,128)(2,1)S(1)}, bf16[1,2048,512]{2,1,0:T(8,128)(2,1)}, u32[]{:S(2)}) copy-start(bf16[1,2048,512]{2,1,0:T(8,128)(2,1)} %param.11) | copy-start | bytes 6291460
  7.2 21.9 %all-gather.4.cloned.1.call-start = ((), (), s32[]{:S(2)}) async-start(), calls=%async_computation.3 | async-start | bytes 1310720 | tf_op jit(solution)/shard_map/all_gather | solution.py:65
  7.9 103.7 %reduce-scatter.2.cloned.1.call-start = ((), (), s32[]{:S(2)}) async-start(), calls=%async_computation.4 | async-start | bytes 5242880 | tf_op jit(solution)/shard_map/reduce_scatter | solution.py:67
  34.6 81.3 %copy-start.1 = (bf16[1,2,32,8192]{3,2,1,0:T(8,128)(2,1)S(1)}, bf16[1,2,32,8192]{3,2,1,0:T(8,128)(2,1)}, u32[]{:S(2)}) copy-start(bf16[1,2,32,8192]{3,2,1,0:T(8,128)(2,1)} %param.9) | copy-start | bytes 3145732
  34.6 84.0 %copy-start.3 = (bf16[1,8192]{1,0:T(2,128)(2,1)S(1)}, bf16[1,8192]{1,0:T(2,128)(2,1)}, u32[]{:S(2)}) copy-start(bf16[1,8192]{1,0:T(2,128)(2,1)} %param.12) | copy-start | bytes 49156
  111.6 18.8 %all-to-all-start = ((bf16[4,2,32,2048]{3,2,1,0:T(8,128)(2,1)}), bf16[4,2,32,2048]{3,2,1,0:T(8,128)(2,1)}, u32[]{:S(2)}, u32[]{:S(2)}) async-start(bf16[4,2,32,2048]{3,2,1,0:T(8,128)(2,1)} %reduce-scatter.2.cloned.1.call-done), calls=%async_computation.1 | async-start | bytes 2097152 | tf_op jit(solution)/shard_map/all_to_all | solution.py:70
  115.8 62.6 %all-gather.6.cloned.1.call-start = ((), (), s32[]{:S(2)}) async-start(), calls=%async_computation.5 | async-start | bytes 3145728 | tf_op jit(solution)/shard_map/all_gather | solution.py:11
  139.6 4.5 %copy-start.2 = (f32[1,2,32,8192]{3,2,1,0:T(8,128)S(1)}, f32[1,2,32,8192]{3,2,1,0:T(8,128)}, u32[]{:S(2)}) copy-start(f32[1,2,32,8192]{3,2,1,0:T(8,128)} %reshape.67) | copy-start | bytes 6291460
  145.6 18.8 %all-to-all-start.1 = ((bf16[4,2,32,2048]{3,2,1,0:T(8,128)(2,1)}), bf16[4,2,32,2048]{3,2,1,0:T(8,128)(2,1)}, u32[]{:S(2)}, u32[]{:S(2)}) async-start(bf16[4,2,32,2048]{3,2,1,0:T(8,128)(2,1)} %get-tuple-element.67), calls=%async_computation.2 | async-start | bytes 2097152 | tf_op jit(solution)/shard_map/all_to_all | solution.py:75
  149.9 110.9 %all-gather.8.cloned.1.call-start = ((), (), s32[]{:S(2)}) async-start(), calls=%async_computation.6 | async-start | bytes 5242880 | tf_op jit(solution)/shard_map/all_gather | solution.py:76
  260.8 4.9 %copy-start.4 = (bf16[4,2,128,2048]{3,2,1,0:T(8,128)(2,1)S(1)}, bf16[4,2,128,2048]{3,2,1,0:T(8,128)(2,1)}, u32[]{:S(2)}) copy-start(bf16[4,2,128,2048]{3,2,1,0:T(8,128)(2,1)} %all-gather.8.cloned.1.call-done) | copy-start | bytes 12582916
  260.8 4.9 %copy-start.5 = (bf16[4,2,128,512]{3,2,1,0:T(8,128)(2,1)S(1)}, bf16[4,2,128,512]{3,2,1,0:T(8,128)(2,1)}, u32[]{:S(2)}) copy-start(bf16[4,2,128,512]{3,2,1,0:T(8,128)(2,1)} %all-gather.4.cloned.1.call-done) | copy-start | bytes 3145732
Sparse Core Ops, SparseCore 0:
  9.6 19.4 all-gather.3
  34.8 76.7 reduce-scatter.1
  145.7 32.6 all-gather.5
  180.0 80.7 all-gather.7

commit v2 on v0

v2 whole, which is shorter than its diff:
```python
import functools

import jax
import jax.numpy as jnp
from jax import lax
from jax.experimental import pallas as pl
from jax.experimental.pallas import tpu as pltpu
from jax.sharding import PartitionSpec as P

MESH = pl.DeviceIdType.MESH
F32 = jnp.float32
BF16 = jnp.bfloat16


def kernel(
    n_dp, n_sec, n_t,
    salt_ref, counter_ref, x_ref, kv_ref, w_ref, gain_ref, top_ref,
    out_ref, wout_ref,
    cot, parts, c_right, c_left, norm, nsend, fin, ng, branch, later, relay, scale,
    cot_send, cot_recv, n_send, n_recv, r_send, r_recv, l_send, l_recv,
    g_send, g_recv, s_send, s_recv,
):
    me = lax.axis_index("dp")
    sec = lax.axis_index("section")
    t = lax.axis_index("tensor")
    rows, width = w_ref.shape
    micro, held, _ = kv_ref.shape
    tok = held // n_t
    chunk = micro * tok
    feats = n_dp * rows
    total_cols = width * n_t

    def at(dp=None, section=None, tensor=None):
        return (
            me if dp is None else dp,
            sec if section is None else section,
            t if tensor is None else tensor,
        )

    def peer(k):
        base = lax.rem(me + 2 * (k // 2), n_dp)
        return base + lax.rem(k, 2) * (1 - 2 * lax.rem(base, 2))

    barrier = pltpu.get_barrier_semaphore()

    def greet(where):
        pl.semaphore_signal(barrier, inc=1, device_id=where, device_id_type=MESH)

    for k in range(1, n_dp):
        greet(at(dp=lax.rem(me + k, n_dp)))

    @pl.when(t > 0)
    def _():
        greet(at(tensor=t - 1))

    @pl.when(t < n_t - 1)
    def _():
        greet(at(tensor=t + 1))

    @pl.when(sec > 0)
    def _():
        greet(at(section=sec - 1))

    @pl.when(sec < n_sec - 1)
    def _():
        greet(at(section=sec + 1))

    for j in range(n_t):
        for m in range(micro):
            cot[me, j, m * tok:(m + 1) * tok, :] = kv_ref[m, j * tok:(j + 1) * tok, :]

    greeted = (
        n_dp - 1
        + jnp.where(t > 0, 1, 0) + jnp.where(t < n_t - 1, 1, 0)
        + jnp.where(sec > 0, 1, 0) + jnp.where(sec < n_sec - 1, 1, 0)
    )
    pl.semaphore_wait(barrier, greeted)

    def cot_copy(source, dest):
        return pltpu.make_async_remote_copy(
            src_ref=cot.at[source], dst_ref=cot.at[source],
            send_sem=cot_send.at[dest], recv_sem=cot_recv.at[source],
            device_id=at(dp=dest), device_id_type=MESH,
        )

    def norm_copy(source, dest):
        return pltpu.make_async_remote_copy(
            src_ref=nsend.at[dest], dst_ref=norm.at[source, t],
            send_sem=n_send.at[dest], recv_sem=n_recv.at[source],
            device_id=at(dp=dest), device_id_type=MESH,
        )

    def grad_copy(source, dest):
        return pltpu.make_async_remote_copy(
            src_ref=fin.at[dest], dst_ref=ng.at[source],
            send_sem=g_send.at[dest], recv_sem=g_recv.at[source],
            device_id=at(dp=dest), device_id_type=MESH,
        )

    def section_copy(dest):
        return pltpu.make_async_remote_copy(
            src_ref=relay, dst_ref=later, send_sem=s_send, recv_sem=s_recv,
            device_id=at(section=dest), device_id_type=MESH,
        )

    for k in range(1, n_dp):
        cot_copy(me, peer(k)).start()

    def make_parts(p):
        left = cot[p].reshape(n_t * chunk, width)
        step = min(512, rows)

        @pl.loop(0, rows // step)
        def _(f):
            cols = pl.ds(pl.multiple_of(f * step, step), step)
            got = lax.dot_general(
                left, w_ref[cols, :], (((1,), (1,)), ((), ())), preferred_element_type=F32
            )
            parts[p, :, :, cols] = got.astype(BF16).reshape(n_t, chunk, step)

    make_parts(me)

    def columns(q):
        return slice(q * rows, (q + 1) * rows)

    def normalise():
        total = jnp.zeros((chunk, 1), F32)
        for q in range(n_dp):
            v = x_ref[:, columns(q)].astype(F32)
            total = total + jnp.sum(v * v, axis=-1, keepdims=True)
        r = lax.rsqrt(total * (1.0 / feats) + 1e-05)
        scale[...] = r
        for q in range(n_dp):
            v = x_ref[:, columns(q)].astype(F32) * r
            nsend[q] = (v * gain_ref[:, columns(q)].astype(F32)).astype(BF16)
        norm[me, t] = nsend[me]
        for k in range(1, n_dp):
            norm_copy(me, peer(k)).start()

    def branch_term():
        r = scale[...]
        total = jnp.zeros((chunk, 1), F32)
        for q in range(n_dp):
            h = ng[q].astype(F32) * gain_ref[:, columns(q)].astype(F32)
            xh = x_ref[:, columns(q)].astype(F32) * r
            total = total + jnp.sum(h * xh, axis=-1, keepdims=True)
        mean = total * (1.0 / feats)
        for q in range(n_dp):
            h = ng[q].astype(F32) * gain_ref[:, columns(q)].astype(F32)
            xh = x_ref[:, columns(q)].astype(F32) * r
            branch[:, columns(q)] = r * (h - xh * mean)

    def emit(with_later):
        for q in range(n_dp):
            v = branch[:, columns(q)]
            if with_later:
                v = v + later[:, columns(q)].astype(F32)
            out_ref[:, columns(q)] = (top_ref[:, columns(q)].astype(F32) + v).astype(BF16)
            relay[:, columns(q)] = v.astype(BF16)

    def weight_grad(p, first):
        right = cot[p].reshape(n_t * chunk, width)
        step = min(128, rows)
        base = (
            salt_ref[0] * jnp.int32(374761393)
            + counter_ref[0] * jnp.int32(668265263)
            + sec * jnp.int32(-1028477379)
            + p * jnp.int32(1274126177)
        )
        cell = (
            lax.broadcasted_iota(jnp.int32, (step, width), 0) * jnp.int32(total_cols)
            + lax.broadcasted_iota(jnp.int32, (step, width), 1)
        ) * jnp.int32(-1640531535)

        @pl.loop(0, rows // step)
        def _(f):
            at_rows = pl.ds(pl.multiple_of(f * step, step), step)
            lhs = norm[p, :, :, at_rows].reshape(n_t * chunk, step)
            term = lax.dot_general(
                lhs, right, (((0,), (0,)), ((), ())), preferred_element_type=F32
            )
            origin = (me * rows + f * step) * total_cols + t * width
            h = cell + (base + origin * jnp.int32(-1640531535))
            h = h ^ lax.shift_right_logical(h, jnp.int32(16))
            h = h * jnp.int32(2146121005)
            h = h ^ lax.shift_right_logical(h, jnp.int32(15))
            h = h * jnp.int32(-2073254261)
            h = h ^ lax.shift_right_logical(h, jnp.int32(16))
            u = lax.shift_right_logical(h, jnp.int32(8)).astype(F32) * (1.0 / 16777216.0)
            moved = (term * (1.0 + (u - 0.5) * 0.5)).astype(BF16).astype(F32)
            wout_ref[at_rows, :] = wout_ref[at_rows, :] + moved

    def line_sum(buf, src, p, j, i, send, recv, dest):
        return pltpu.make_async_remote_copy(
            src_ref=src.at[p, j], dst_ref=buf.at[p, j],
            send_sem=send.at[i], recv_sem=recv.at[i],
            device_id=at(tensor=dest), device_id_type=MESH,
        )

    def line_norm(p, j, i, send, recv, dest):
        return pltpu.make_async_remote_copy(
            src_ref=norm.at[p, j], dst_ref=norm.at[p, j],
            send_sem=send.at[i], recv_sem=recv.at[i],
            device_id=at(tensor=dest), device_id_type=MESH,
        )

    sides = (
        (c_right, r_send, r_recv, -1),
        (c_left, l_send, l_recv, 1),
    )

    def each_side(fn, s):
        for buf, send, recv, back in sides:
            if back < 0:
                j, has_in, has_out = n_t - 1 - s, t > 0, t < n_t - 1
                is_sum, lands_sum = j > t, j >= t
            else:
                j, has_in, has_out = s, t < n_t - 1, t > 0
                is_sum, lands_sum = j < t, j <= t
            fn(buf, send, recv, t + back, t - back, j, has_in, has_out, is_sum, lands_sum)

    last_sum = jnp.where((t == 0) | (t == n_t - 1), 0, jnp.maximum(t, n_t - 1 - t))

    def one(i, carry):
        s = i // n_dp
        k = lax.rem(i, n_dp)
        p = peer(k)

        @pl.when((s == 0) & (k > 0))
        def _():
            cot_copy(p, me).wait_recv()
            make_parts(p)

        @pl.when((s == 1) & (k > 0))
        def _():
            norm_copy(p, me).wait_recv()

        def side(buf, send, recv, source, dest, j, has_in, has_out, is_sum, lands_sum):
            @pl.when(has_in & lands_sum)
            def _():
                line_sum(buf, buf, p, j, i, send, recv, source).wait_recv()

            @pl.when(has_in & jnp.logical_not(lands_sum))
            def _():
                line_norm(p, j, i, send, recv, source).wait_recv()

            @pl.when(has_out & is_sum & has_in)
            def _():
                buf[p, j] = (buf[p, j].astype(F32) + parts[p, j].astype(F32)).astype(BF16)
                line_sum(buf, buf, p, j, i, send, recv, dest).start()

            @pl.when(has_out & is_sum & jnp.logical_not(has_in))
            def _():
                line_sum(buf, parts, p, j, i, send, recv, dest).start()

            @pl.when(has_out & jnp.logical_not(is_sum))
            def _():
                line_norm(p, j, i, send, recv, dest).start()

        each_side(side, s)

        @pl.when(i == 0)
        def _():
            normalise()
            wout_ref[...] = jnp.zeros_like(wout_ref)

        @pl.when(s == last_sum)
        def _():
            fin[p] = parts[p, t]

            @pl.when(t > 0)
            def _():
                fin[p] = (fin[p].astype(F32) + c_right[p, t].astype(F32)).astype(BF16)

            @pl.when(t < n_t - 1)
            def _():
                fin[p] = (fin[p].astype(F32) + c_left[p, t].astype(F32)).astype(BF16)

            @pl.when(k == 0)
            def _():
                ng[me] = fin[me]

            @pl.when(k > 0)
            def _():
                grad_copy(me, p).start()

        @pl.when((s == n_t - 1) & (k == min(1, n_dp - 1)))
        def _():
            for kk in range(1, n_dp):
                grad_copy(peer(kk), me).wait_recv()
            branch_term()

            @pl.when(sec == n_sec - 1)
            def _():
                emit(False)

                @pl.when(sec > 0)
                def _():
                    section_copy(sec - 1).start()

        @pl.when(s == n_t - 1)
        def _():
            weight_grad(p, k == 0)

        return carry

    lax.fori_loop(0, n_t * n_dp, one, 0)

    @pl.when(sec < n_sec - 1)
    def _():
        section_copy(sec + 1).wait_recv()
        emit(True)

        @pl.when(sec > 0)
        def _():
            section_copy(sec - 1).start()

    def drain(i, carry):
        s = i // n_dp
        p = peer(lax.rem(i, n_dp))

        def side(buf, send, recv, source, dest, j, has_in, has_out, is_sum, lands_sum):
            @pl.when(has_out & is_sum & has_in)
            def _():
                line_sum(buf, buf, p, j, i, send, recv, dest).wait_send()

            @pl.when(has_out & is_sum & jnp.logical_not(has_in))
            def _():
                line_sum(buf, parts, p, j, i, send, recv, dest).wait_send()

            @pl.when(has_out & jnp.logical_not(is_sum))
            def _():
                line_norm(p, j, i, send, recv, dest).wait_send()

        each_side(side, s)
        return carry

    lax.fori_loop(0, n_t * n_dp, drain, 0)
    for k in range(1, n_dp):
        cot_copy(me, peer(k)).wait_send()
        norm_copy(me, peer(k)).wait_send()
        grad_copy(me, peer(k)).wait_send()

    @pl.when(sec > 0)
    def _():
        section_copy(sec - 1).wait_send()


def shards(saved_input, kv_grad, kv_weight, norm_gain, top_grad, noise_salt, step_counter):
    n_dp, n_sec, n_t = (lax.axis_size(a) for a in ("dp", "section", "tensor"))
    _, micro, tok, feats = saved_input.shape
    rows, width = kv_weight.shape[1:]
    chunk = micro * tok
    vmem = pl.BlockSpec(memory_space=pltpu.VMEM)
    smem = pl.BlockSpec(memory_space=pltpu.SMEM)
    dma = pltpu.SemaphoreType.DMA
    grads, weights = pl.pallas_call(
        functools.partial(kernel, n_dp, n_sec, n_t),
        out_shape=(
            jax.ShapeDtypeStruct((chunk, feats), BF16),
            jax.ShapeDtypeStruct((rows, width), F32),
        ),
        in_specs=[smem, smem] + [vmem] * 5,
        out_specs=(vmem, vmem),
        scratch_shapes=[
            pltpu.VMEM((n_dp, n_t, chunk, width), BF16),
            pltpu.VMEM((n_dp, n_t, chunk, rows), BF16),
            pltpu.VMEM((n_dp, n_t, chunk, rows), BF16),
            pltpu.VMEM((n_dp, n_t, chunk, rows), BF16),
            pltpu.VMEM((n_dp, n_t, chunk, rows), BF16),
            pltpu.VMEM((n_dp, chunk, rows), BF16),
            pltpu.VMEM((n_dp, chunk, rows), BF16),
            pltpu.VMEM((n_dp, chunk, rows), BF16),
            pltpu.VMEM((chunk, feats), F32),
            pltpu.VMEM((chunk, feats), BF16),
            pltpu.VMEM((chunk, feats), BF16),
            pltpu.VMEM((chunk, 1), F32),
            dma((n_dp,)), dma((n_dp,)), dma((n_dp,)), dma((n_dp,)),
            dma((n_t * n_dp,)), dma((n_t * n_dp,)), dma((n_t * n_dp,)), dma((n_t * n_dp,)),
            dma((n_dp,)), dma((n_dp,)), dma, dma,
        ],
        compiler_params=pltpu.CompilerParams(
            collective_id=0, has_side_effects=True, vmem_limit_bytes=56 * 1024 * 1024
        ),
    )(
        noise_salt, step_counter,
        saved_input.reshape(chunk, feats), kv_grad[0], kv_weight[0], norm_gain,
        top_grad.reshape(chunk, feats),
    )
    return grads.reshape(1, micro, tok, feats), weights[None]


def solution(mesh):
    placed = (
        P("section", None, ("dp", "tensor"), None),
        P("section", None, "dp", "tensor"),
        P("section", "dp", "tensor"),
        P("section", None),
        P(None, ("dp", "tensor"), None),
        P(),
        P(),
    )
    return jax.shard_map(
        shards,
        mesh=mesh,
        in_specs=placed,
        out_specs=(P("section", None, ("dp", "tensor"), None), P("section", "dp", "tensor")),
        check_vma=False,
    )
```

time: 359 us -> 597 us (1.66); the launches traced: 359 us -> 590 us
  Pallas kernels: 0 us -> 581 us
  waiting for transfers between devices: 304 us -> 0 us
  matrix products: 24.2 us -> 0 us
  other arithmetic: 14 us -> 0 us
  between operations: 15.1 us -> 1.93 us
    pallas_call x0 -> x1, Pallas kernels: none -> 581 us  [shards(): pl.pallas_call(functools.partial(kernel, n_dp, n_sec, n_t), out_shape=(ja...]
    all_gather x3 -> x0, waiting for transfers between devices: 158 us -> none  [the longest x1 78.4 us: shards(): normed_all = lax.all_gather(normed_values, 'tensor', axis=1, tiled=True)]
    reduce_scatter x2 -> x0, waiting for transfers between devices: 145 us -> none  [the longest x1 75.4 us: shards(): lax.psum_scatter(partial_grad.astype(jnp.bfloat16), 'tensor', scatter_dim...]
    dot_general x2 -> x0, matrix products: 24.2 us -> none  [the longest x1 16.4 us: shards(): jnp.einsum('mtd,mtk->dk', normed_all, cotan, preferred_element_type=jnp.f...]
    broadcast_in_dim x2 -> x0, other arithmetic: 7.47 us -> none  [shards(): return (grad_in[None], wsum[None])]
  transfers between devices with their start and end apart: 5 -> 0, of which waited for: 5 -> 0; matrix products, arithmetic and copies ran while one was open for 7% -> 0% of each run, Pallas kernels for 0% -> 0%
where the time goes in v2:
time: 597 us; the launch traced here: 590 us
  Pallas kernels  581 us (97%)
  local copies, waits for them, and re-layouts  6.9 us (1%)
    pallas_call x1, Pallas kernels, shards(): pl.pallas_call(functools.partial(kernel, n_dp, n_sec, n_t), out_shape=(ja...  581 us

profile of v2, /device:TPU:0, one launch (start us, length us, event | category | flops | bytes accessed | tf_op | source)
XLA Modules:
  0.0 589.6 jit_solution(9100287518744459653)
XLA Ops:
  1.9 580.8 %shard_map.86 = (bf16[64,8192]{1,0:T(8,128)(2,1)}, f32[2048,512]{1,0:T(8,128)}) custom-call(s32[1]{0:T(128)S(6)} %copy.11.salt_ref, s32[1]{0:T(128)S(6)} %copy.12.counter_ref, bf16[64,8192]{1,0:T(8,128)(2,1)} %bitcast.8, bf16[2,128,512]{2,1,0:T(8,128)(2,1)} %bitcast.11, bf16[2048,512]{1,0:T(8,128)(2,1)} %bitcast.7, bf16[1,8192]{1,0:T(2,128)(2,1)} %gain_ref.1, ...), custom_call_target="tpu_custom_call" | custom-call | tf_op jit(solution)/shard_map/pallas_call | solution.py:357
  582.7 2.3 copy.13
  585.0 4.6 copy.14

commit v3 on v2

--- a/solution.py
+++ b/solution.py
@@ -8,6 +8,7 @@
 from jax.sharding import PartitionSpec as P
 
 MESH = pl.DeviceIdType.MESH
+HOP = 2
 F32 = jnp.float32
 BF16 = jnp.bfloat16
 
@@ -158,7 +159,7 @@
             out_ref[:, columns(q)] = (top_ref[:, columns(q)].astype(F32) + v).astype(BF16)
             relay[:, columns(q)] = v.astype(BF16)
 
-    def weight_grad(p, first):
+    def weight_grad(p):
         right = cot[p].reshape(n_t * chunk, width)
         step = min(128, rows)
         base = (
@@ -209,33 +210,41 @@
         (c_left, l_send, l_recv, 1),
     )
 
-    def each_side(fn, s):
+    def turns(fn, c):
         for buf, send, recv, back in sides:
-            if back < 0:
-                j, has_in, has_out = n_t - 1 - s, t > 0, t < n_t - 1
-                is_sum, lands_sum = j > t, j >= t
-            else:
-                j, has_in, has_out = s, t < n_t - 1, t > 0
-                is_sum, lands_sum = j < t, j <= t
-            fn(buf, send, recv, t + back, t - back, j, has_in, has_out, is_sum, lands_sum)
-
-    last_sum = jnp.where((t == 0) | (t == n_t - 1), 0, jnp.maximum(t, n_t - 1 - t))
-
-    def one(i, carry):
-        s = i // n_dp
-        k = lax.rem(i, n_dp)
-        p = peer(k)
-
-        @pl.when((s == 0) & (k > 0))
-        def _():
-            cot_copy(p, me).wait_recv()
-            make_parts(p)
-
-        @pl.when((s == 1) & (k > 0))
-        def _():
-            norm_copy(p, me).wait_recv()
-
-        def side(buf, send, recv, source, dest, j, has_in, has_out, is_sum, lands_sum):
+            lag = HOP * t if back < 0 else HOP * (n_t - 1 - t)
+
+            @pl.when((c >= lag) & (c < lag + n_t * n_dp))
+            def _():
+                i = c - lag
+                s = i // n_dp
+                p = peer(lax.rem(i, n_dp))
+                if back < 0:
+                    j, has_in, has_out = n_t - 1 - s, t > 0, t < n_t - 1
+                    is_sum, lands_sum = j > t, j >= t
+                else:
+                    j, has_in, has_out = s, t < n_t - 1, t > 0
+                    is_sum, lands_sum = j < t, j <= t
+                fn(buf, send, recv, t + back, t - back, j, has_in, has_out, is_sum, lands_sum, p, i)
+
+    total_messages = n_t * n_dp
+    sum_turn = jnp.maximum(
+        jnp.where(t > 0, (n_t - 1 - t) * n_dp + HOP * t, 0),
+        jnp.where(t < n_t - 1, t * n_dp + HOP * (n_t - 1 - t), 0),
+    )
+    weight_turn = (n_t - 1) * n_dp + HOP * jnp.maximum(t, n_t - 1 - t)
+
+    def one(c, carry):
+        @pl.when((c > 0) & (c < n_dp))
+        def _():
+            cot_copy(peer(c), me).wait_recv()
+            make_parts(peer(c))
+
+        @pl.when((c > n_dp) & (c < 2 * n_dp))
+        def _():
+            norm_copy(peer(c - n_dp), me).wait_recv()
+
+        def side(buf, send, recv, source, dest, j, has_in, has_out, is_sum, lands_sum, p, i):
             @pl.when(has_in & lands_sum)
             def _():
                 line_sum(buf, buf, p, j, i, send, recv, source).wait_recv()
@@ -257,15 +266,17 @@
             def _():
                 line_norm(p, j, i, send, recv, dest).start()
 
-        each_side(side, s)
-
-        @pl.when(i == 0)
+        turns(side, c)
+
+        @pl.when(c == 0)
         def _():
             normalise()
             wout_ref[...] = jnp.zeros_like(wout_ref)
 
-        @pl.when(s == last_sum)
-        def _():
+        @pl.when((c >= sum_turn) & (c < sum_turn + n_dp))
+        def _():
+            k = c - sum_turn
+            p = peer(k)
             fin[p] = parts[p, t]
 
             @pl.when(t > 0)
@@ -284,7 +295,7 @@
             def _():
                 grad_copy(me, p).start()
 
-        @pl.when((s == n_t - 1) & (k == min(1, n_dp - 1)))
+        @pl.when(c == sum_turn + n_dp + 1)
         def _():
             for kk in range(1, n_dp):
                 grad_copy(peer(kk), me).wait_recv()
@@ -298,13 +309,13 @@
                 def _():
                     section_copy(sec - 1).start()
 
-        @pl.when(s == n_t - 1)
-        def _():
-            weight_grad(p, k == 0)
+        @pl.when((c >= weight_turn) & (c < weight_turn + n_dp))
+        def _():
+            weight_grad(peer(c - weight_turn))
 
         return carry
 
-    lax.fori_loop(0, n_t * n_dp, one, 0)
+    lax.fori_loop(0, total_messages + HOP * (n_t - 1), one, 0)
 
     @pl.when(sec < n_sec - 1)
     def _():
@@ -315,11 +326,8 @@
         def _():
             section_copy(sec - 1).start()
 
-    def drain(i, carry):
-        s = i // n_dp
-        p = peer(lax.rem(i, n_dp))
-
-        def side(buf, send, recv, source, dest, j, has_in, has_out, is_sum, lands_sum):
+    def drain(c, carry):
+        def side(buf, send, recv, source, dest, j, has_in, has_out, is_sum, lands_sum, p, i):
             @pl.when(has_out & is_sum & has_in)
             def _():
                 line_sum(buf, buf, p, j, i, send, recv, dest).wait_send()
@@ -332,10 +340,10 @@
             def _():
                 line_norm(p, j, i, send, recv, dest).wait_send()
 
-        each_side(side, s)
+        turns(side, c)
         return carry
 
-    lax.fori_loop(0, n_t * n_dp, drain, 0)
+    lax.fori_loop(0, total_messages + HOP * (n_t - 1), drain, 0)
     for k in range(1, n_dp):
         cot_copy(me, peer(k)).wait_send()
         norm_copy(me, peer(k)).wait_send()

time: 597 us -> 135 us (0.23); the launches traced: 590 us -> 135 us
  Pallas kernels: 581 us -> 126 us
    pallas_call x1, Pallas kernels: 581 us -> 126 us  [shards(): pl.pallas_call(functools.partial(kernel, n_dp, n_sec, n_t), out_shape=(ja...]
where the time goes in v3:
time: 135 us
  Pallas kernels  126 us (93%)
  local copies, waits for them, and re-layouts  6.9 us (5%)
  between operations  1.93 us (1%)
    pallas_call x1, Pallas kernels, shards(): pl.pallas_call(functools.partial(kernel, n_dp, n_sec, n_t), out_shape=(ja...  126 us
    unnamed x2, local copies, waits for them, and re-layouts  6.9 us

profile of v3, /device:TPU:0, one launch (start us, length us, event | category | flops | bytes accessed | tf_op | source)
XLA Modules:
  0.0 134.8 jit_solution(1866876330448571645)
XLA Ops:
  1.9 126.0 %shard_map.86 = (bf16[64,8192]{1,0:T(8,128)(2,1)}, f32[2048,512]{1,0:T(8,128)}) custom-call(s32[1]{0:T(128)S(6)} %copy.11.salt_ref, s32[1]{0:T(128)S(6)} %copy.12.counter_ref, bf16[64,8192]{1,0:T(8,128)(2,1)} %bitcast.8, bf16[2,128,512]{2,1,0:T(8,128)(2,1)} %bitcast.11, bf16[2048,512]{1,0:T(8,128)(2,1)} %bitcast.7, bf16[1,8192]{1,0:T(2,128)(2,1)} %gain_ref.1, ...), custom_call_target="tpu_custom_call" | custom-call | tf_op jit(solution)/shard_map/pallas_call | solution.py:365
  127.9 2.3 %copy.13 = bf16[1,2,32,8192]{3,2,1,0:T(8,128)(2,1)} copy(bf16[1,2,32,8192]{3,2,1,0:T(8,128)(2,1)} %bitcast.10) | data formatting | bytes 2097152
  130.2 4.6 %copy.14 = f32[1,2048,512]{2,1,0:T(8,128)} copy(f32[1,2048,512]{2,1,0:T(8,128)} %bitcast.6) | data formatting | bytes 8388608

commit v4 on v3

--- a/solution.py
+++ b/solution.py
@@ -8,7 +8,8 @@
 from jax.sharding import PartitionSpec as P
 
 MESH = pl.DeviceIdType.MESH
-HOP = 2
+CUT = 2
+HOP = 3
 F32 = jnp.float32
 BF16 = jnp.bfloat16
 
@@ -161,7 +162,7 @@
 
     def weight_grad(p):
         right = cot[p].reshape(n_t * chunk, width)
-        step = min(128, rows)
+        step = min(256, rows)
         base = (
             salt_ref[0] * jnp.int32(374761393)
             + counter_ref[0] * jnp.int32(668265263)
@@ -191,16 +192,22 @@
             moved = (term * (1.0 + (u - 0.5) * 0.5)).astype(BF16).astype(F32)
             wout_ref[at_rows, :] = wout_ref[at_rows, :] + moved
 
+    part = chunk // CUT
+    n_k = n_dp * CUT
+
+    def piece(i):
+        return pl.ds(pl.multiple_of(lax.rem(i, CUT) * part, part), part)
+
     def line_sum(buf, src, p, j, i, send, recv, dest):
         return pltpu.make_async_remote_copy(
-            src_ref=src.at[p, j], dst_ref=buf.at[p, j],
+            src_ref=src.at[p, j, piece(i)], dst_ref=buf.at[p, j, piece(i)],
             send_sem=send.at[i], recv_sem=recv.at[i],
             device_id=at(tensor=dest), device_id_type=MESH,
         )
 
     def line_norm(p, j, i, send, recv, dest):
         return pltpu.make_async_remote_copy(
-            src_ref=norm.at[p, j], dst_ref=norm.at[p, j],
+            src_ref=norm.at[p, j, piece(i)], dst_ref=norm.at[p, j, piece(i)],
             send_sem=send.at[i], recv_sem=recv.at[i],
             device_id=at(tensor=dest), device_id_type=MESH,
         )
@@ -214,11 +221,11 @@
         for buf, send, recv, back in sides:
             lag = HOP * t if back < 0 else HOP * (n_t - 1 - t)
 
-            @pl.when((c >= lag) & (c < lag + n_t * n_dp))
+            @pl.when((c >= lag) & (c < lag + n_t * n_k))
             def _():
                 i = c - lag
-                s = i // n_dp
-                p = peer(lax.rem(i, n_dp))
+                s = i // n_k
+                p = peer(lax.rem(i, n_k) // CUT)
                 if back < 0:
                     j, has_in, has_out = n_t - 1 - s, t > 0, t < n_t - 1
                     is_sum, lands_sum = j > t, j >= t
@@ -227,22 +234,22 @@
                     is_sum, lands_sum = j < t, j <= t
                 fn(buf, send, recv, t + back, t - back, j, has_in, has_out, is_sum, lands_sum, p, i)
 
-    total_messages = n_t * n_dp
+    total_messages = n_t * n_k
     sum_turn = jnp.maximum(
-        jnp.where(t > 0, (n_t - 1 - t) * n_dp + HOP * t, 0),
-        jnp.where(t < n_t - 1, t * n_dp + HOP * (n_t - 1 - t), 0),
-    )
-    weight_turn = (n_t - 1) * n_dp + HOP * jnp.maximum(t, n_t - 1 - t)
+        jnp.where(t > 0, (n_t - 1 - t) * n_k + HOP * t, 0),
+        jnp.where(t < n_t - 1, t * n_k + HOP * (n_t - 1 - t), 0),
+    )
+    weight_turn = (n_t - 1) * n_k + HOP * jnp.maximum(t, n_t - 1 - t)
 
     def one(c, carry):
-        @pl.when((c > 0) & (c < n_dp))
-        def _():
-            cot_copy(peer(c), me).wait_recv()
-            make_parts(peer(c))
-
-        @pl.when((c > n_dp) & (c < 2 * n_dp))
-        def _():
-            norm_copy(peer(c - n_dp), me).wait_recv()
+        @pl.when((c > 0) & (c < n_k) & (lax.rem(c, CUT) == 0))
+        def _():
+            cot_copy(peer(c // CUT), me).wait_recv()
+            make_parts(peer(c // CUT))
+
+        @pl.when((c > n_k) & (c < 2 * n_k) & (lax.rem(c, CUT) == 0))
+        def _():
+            norm_copy(peer((c - n_k) // CUT), me).wait_recv()
 
         def side(buf, send, recv, source, dest, j, has_in, has_out, is_sum, lands_sum, p, i):
             @pl.when(has_in & lands_sum)
@@ -255,7 +262,10 @@
 
             @pl.when(has_out & is_sum & has_in)
             def _():
-                buf[p, j] = (buf[p, j].astype(F32) + parts[p, j].astype(F32)).astype(BF16)
+                at_piece = piece(i)
+                buf[p, j, at_piece] = (
+                    buf[p, j, at_piece].astype(F32) + parts[p, j, at_piece].astype(F32)
+                ).astype(BF16)
                 line_sum(buf, buf, p, j, i, send, recv, dest).start()
 
             @pl.when(has_out & is_sum & jnp.logical_not(has_in))
@@ -273,9 +283,9 @@
             normalise()
             wout_ref[...] = jnp.zeros_like(wout_ref)
 
-        @pl.when((c >= sum_turn) & (c < sum_turn + n_dp))
-        def _():
-            k = c - sum_turn
+        @pl.when((c >= sum_turn) & (c < sum_turn + n_k) & (lax.rem(c - sum_turn + CUT * n_k, CUT) == CUT - 1))
+        def _():
+            k = (c - sum_turn) // CUT
             p = peer(k)
             fin[p] = parts[p, t]
 
@@ -295,7 +305,7 @@
             def _():
                 grad_copy(me, p).start()
 
-        @pl.when(c == sum_turn + n_dp + 1)
+        @pl.when(c == sum_turn + n_k + 2)
         def _():
             for kk in range(1, n_dp):
                 grad_copy(peer(kk), me).wait_recv()
@@ -309,9 +319,9 @@
                 def _():
                     section_copy(sec - 1).start()
 
-        @pl.when((c >= weight_turn) & (c < weight_turn + n_dp))
-        def _():
-            weight_grad(peer(c - weight_turn))
+        @pl.when((c >= weight_turn) & (c < weight_turn + n_k) & (lax.rem(c - weight_turn + 2 * total_messages, CUT) == CUT - 1))
+        def _():
+            weight_grad(peer((c - weight_turn) // CUT))
 
         return carry
 
@@ -384,7 +394,7 @@
             pltpu.VMEM((chunk, feats), BF16),
             pltpu.VMEM((chunk, 1), F32),
             dma((n_dp,)), dma((n_dp,)), dma((n_dp,)), dma((n_dp,)),
-            dma((n_t * n_dp,)), dma((n_t * n_dp,)), dma((n_t * n_dp,)), dma((n_t * n_dp,)),
+            dma((n_t * n_dp * CUT,)), dma((n_t * n_dp * CUT,)), dma((n_t * n_dp * CUT,)), dma((n_t * n_dp * CUT,)),
             dma((n_dp,)), dma((n_dp,)), dma, dma,
         ],
         compiler_params=pltpu.CompilerParams(

time: 135 us -> 132 us (0.978)
  Pallas kernels: 126 us -> 122 us
    pallas_call x1, Pallas kernels: 126 us -> 122 us  [shards(): pl.pallas_call(functools.partial(kernel, n_dp, n_sec, n_t), out_shape=(ja...]
where the time goes in v4:
time: 132 us; the launch traced here: 131 us
  Pallas kernels  122 us (92%)
  local copies, waits for them, and re-layouts  6.9 us (5%)
  between operations  1.93 us (1%)
    pallas_call x1, Pallas kernels, shards(): pl.pallas_call(functools.partial(kernel, n_dp, n_sec, n_t), out_shape=(ja...  122 us
    unnamed x2, local copies, waits for them, and re-layouts  6.9 us

profile of v4, /device:TPU:0, one launch (start us, length us, event | category | flops | bytes accessed | tf_op | source)
XLA Modules:
  0.0 131.3 jit_solution(16933360936216927586)
XLA Ops:
  1.9 122.5 %shard_map.86 = (bf16[64,8192]{1,0:T(8,128)(2,1)}, f32[2048,512]{1,0:T(8,128)}) custom-call(s32[1]{0:T(128)S(6)} %copy.11.salt_ref, s32[1]{0:T(128)S(6)} %copy.12.counter_ref, bf16[64,8192]{1,0:T(8,128)(2,1)} %bitcast.8, bf16[2,128,512]{2,1,0:T(8,128)(2,1)} %bitcast.11, bf16[2048,512]{1,0:T(8,128)(2,1)} %bitcast.7, bf16[1,8192]{1,0:T(2,128)(2,1)} %gain_ref.1, ...), custom_call_target="tpu_custom_call" | custom-call | tf_op jit(solution)/shard_map/pallas_call | solution.py:375
  124.4 2.3 %copy.13 = bf16[1,2,32,8192]{3,2,1,0:T(8,128)(2,1)} copy(bf16[1,2,32,8192]{3,2,1,0:T(8,128)(2,1)} %bitcast.10) | data formatting | bytes 2097152
  126.7 4.6 %copy.14 = f32[1,2048,512]{2,1,0:T(8,128)} copy(f32[1,2048,512]{2,1,0:T(8,128)} %bitcast.6) | data formatting | bytes 8388608
